TPU v7x, 256 devices: a whole 4x4x8 slice. The times are simulated.
256 devices in a mesh: pb: 64 (over z, x, core), ka: 4 (over y).
Axes of the slice: x: 4, y: 4, z: 8, core: 2. Of those that a mesh axis runs over, the one named last changes fastest.
Arguments:
- queries: bfloat16 [65536, 512], P('pb'), may hold values from -80 to 80
- key_cache: bfloat16 [65536, 128], P(('ka', 'pb')), may hold values from -4.1 to 4.1
- value_cache: bfloat16 [65536, 128], P(('ka', 'pb')), may hold values from -4 to 4
- block_list: int32 [512, 32], P('pb'), may hold values from 0 to 511, as said below
- block_count: int32 [512], P('pb'), may hold values from 1 to 32, as said below
Outputs:
- attended: bfloat16 [65536, 512], P(('pb', 'ka'))
Inputs may be any that keep to these rules, and one draw needn't show every extreme that they name: `block_list`: entries of row qb before block_count[qb] are distinct blocks at most qb, and qb itself is among them. They are the blocks v at most qb of one set of 16 vertical blocks, then the blocks qb - o at least 0 (and not already listed) of one set of 16 slash offsets; both sets contain 0 and lie below 128. Later entries equal qb. `block_count`: the number of distinct listed blocks of each query block.
All inputs are finite; a program needn't handle non-finite values.
Results may differ from a plain program's by a relative error of at most 0.0046.
Values may be sent and summed in bfloat16 or wider, within the bound.
A program may use at most 128 MiB of HBM per device.

v0:
```python
import math
import jax
import jax.numpy as jnp
from jax import lax
from jax.sharding import PartitionSpec as P

HD = 128
QH = 4
BLK = 128
LIST = 32
masked_score = -1e30


def merged(shard, axis, combine):
    everything = jax.tree.map(lambda part: lax.all_gather(part, axis), shard)
    initial = jax.tree.map(lambda part: part[0], everything)

    def lap(k, so_far):
        return combine(so_far, jax.tree.map(lambda part: part[k], everything))

    return lax.fori_loop(1, lax.axis_size(axis), lap, initial)


def combine(first, second):
    peak_first, sum_first, out_first = first
    peak_second, sum_second, out_second = second
    peak_both = jnp.maximum(peak_first, peak_second)
    factor_first = jnp.exp(peak_first - peak_both)
    factor_second = jnp.exp(peak_second - peak_both)
    sum_both = factor_first * sum_first + factor_second * sum_second
    out_both = (
        jnp.repeat(factor_first, HD, axis=1) * out_first
        + jnp.repeat(factor_second, HD, axis=1) * out_second
    )
    return (peak_both, sum_both, out_both)


def shards(queries, key_cache, value_cache, block_list, block_count):
    shard_keys, shard_values = (
        lax.all_gather(key_cache, "pb", axis=0, tiled=True),
        lax.all_gather(value_cache, "pb", axis=0, tiled=True),
    )
    group_index = lax.axis_index("pb")
    shard_index = lax.axis_index("ka")
    ka_width = lax.axis_size("ka")
    score_scale = 1.0 / math.sqrt(HD)
    shard_width = shard_keys.shape[0] // BLK
    local_blocks = queries.shape[0] // BLK
    first_block = shard_index * shard_width
    all_key_tiles = shard_keys.reshape(shard_width, BLK, HD)
    all_value_tiles = shard_values.reshape(shard_width, BLK, HD)
    slot_ids = jnp.arange(LIST, dtype=jnp.int32)
    position = jnp.arange(BLK, dtype=jnp.int32)

    def one_block(block_pos):
        query_rows = lax.dynamic_slice_in_dim(queries, block_pos * BLK, BLK, 0).reshape(BLK, QH, HD)
        listed = lax.dynamic_index_in_dim(block_list, block_pos, 0, keepdims=False)
        live_count = lax.dynamic_index_in_dim(block_count, block_pos, 0, keepdims=False)
        global_pos = group_index * local_blocks + block_pos
        live_slot = slot_ids < live_count
        local_ids = listed - first_block
        tile_live = live_slot & (local_ids >= 0) & (local_ids < shard_width)
        picked = jnp.clip(local_ids, 0, shard_width - 1)
        key_tiles = all_key_tiles[picked]
        value_tiles = all_value_tiles[picked]
        scores = (
            jnp.einsum("qhd,skd->hqsk", query_rows, key_tiles, preferred_element_type=jnp.float32)
            * score_scale
        )
        earlier = (listed < global_pos)[None, :, None]
        diagonal = (listed == global_pos)[None, :, None] & (
            position[None, None, :] <= position[:, None, None]
        )
        valid = tile_live[None, :, None] & (earlier | diagonal)
        masked = jnp.where(valid[None], scores, masked_score)
        peak_row = jnp.max(masked, axis=(2, 3))
        weights = jnp.where(valid[None], jnp.exp(scores - peak_row[..., None, None]), 0.0)
        weight_sum = jnp.sum(weights, axis=(2, 3))
        partial_out = jnp.einsum(
            "hqsk,skd->qhd",
            weights.astype(jnp.bfloat16),
            value_tiles,
            preferred_element_type=jnp.float32,
        )
        return (peak_row.T, weight_sum.T, partial_out.reshape(BLK, QH * HD))

    peaks, sums, outputs = lax.map(one_block, jnp.arange(local_blocks, dtype=jnp.int32))
    peaks = peaks.reshape(local_blocks * BLK, QH)
    sums = sums.reshape(local_blocks * BLK, QH)
    outputs = outputs.reshape(local_blocks * BLK, QH * HD)
    merged_peak, merged_sum, merged_out = merged((peaks, sums, outputs), "ka", combine)
    owned = merged_out.shape[0] // ka_width
    out_share = lax.dynamic_slice_in_dim(merged_out, shard_index * owned, owned, 0)
    sum_share = lax.dynamic_slice_in_dim(merged_sum, shard_index * owned, owned, 0)
    return (out_share / jnp.repeat(sum_share, HD, axis=1)).astype(jnp.bfloat16)


def solution(mesh):
    placed = (P("pb", None), P(("ka", "pb"), None), P(("ka", "pb"), None), P("pb", None), P("pb"))
    return jax.shard_map(
        shards, mesh=mesh, in_specs=placed, out_specs=P(("pb", "ka"), None), check_vma=False
    )
```

profile of v0, /device:TPU:1, one launch (start us, length us, event | category | flops | bytes accessed | tf_op | source)
XLA Modules:
  0.0 492.1 jit_solution(4541151159910000270)
XLA Ops:
  8.1 85.3 %all-gather.4.cloned.1.call-done = bf16[16384,128]{1,0:T(8,128)(2,1)} async-done(((bf16[256,128]{1,0:T(8,128)(2,1)}), bf16[16384,128]{1,0:T(8,128)(2,1)}) %all-gather.4.cloned.1.call-update) | async-done | bytes 4194320 | tf_op jit(solution)/shard_map/all_gather | solution.py:40
  93.3 79.1 %all-gather.6.cloned.1.call-done = bf16[16384,128]{1,0:T(8,128)(2,1)} async-done(((bf16[256,128]{1,0:T(8,128)(2,1)}), bf16[16384,128]{1,0:T(8,128)(2,1)}) %all-gather.6.cloned.1.call-update) | async-done | bytes 4194320 | tf_op jit(solution)/shard_map/all_gather | solution.py:41
  172.4 201.8 %while.37 = (s32[]{:T(128)}, f32[8,128,4]{1,2,0:T(4,128)S(1)}, f32[8,128,4]{1,2,0:T(4,128)S(1)}, f32[8,128,512]{2,1,0:T(8,128)}, s32[8]{0:T(128)S(1)}, /*index=5...) while((s32[]{:T(128)}, f32[8,128,4]{1,2,0:T(4,128)S(1)}, ...), condition=%wide.region_3.4_spmd.clone, body=%wide.region_0.3_spmd.clone.sunk | while | flops 1098400256 | bytes 69129872 | solution.py:87
  181.2 2.9 gather_fusion
  191.6 5.2 %fusion.41 = f32[128,4,128,1]{2,0,1,3:T(8,128)S(1)} fusion(f32[32,128,128,4]{2,1,3,0:T(8,128)} %copy-done, f32[4,128]{1,0:T(4,128)S(1)} %get-tuple-element.581, pred[128,32,128]{0,2,1:T(8,128)(4,1)S(1)} %or_and_fusion.2, bf16[32,128,128]{2,1,0:T(8,128)(2,1)S(1)} %gather_fusion.1), kind=kOutput, calls=%fused_computation.20.clone.1 | convolution fusion | flops 545259520 | bytes 10225664 | tf_op jit(solution)/shard_map/while/body/eval_jaxpr/hqsk,skd->qhd/dot_general | solution.py:79
  206.4 2.9 gather_fusion
  216.8 5.2 %fusion.41 = f32[128,4,128,1]{2,0,1,3:T(8,128)S(1)} fusion(f32[32,128,128,4]{2,1,3,0:T(8,128)} %copy-done, f32[4,128]{1,0:T(4,128)S(1)} %get-tuple-element.581, pred[128,32,128]{0,2,1:T(8,128)(4,1)S(1)} %or_and_fusion.2, bf16[32,128,128]{2,1,0:T(8,128)(2,1)S(1)} %gather_fusion.1), kind=kOutput, calls=%fused_computation.20.clone.1 | convolution fusion | flops 545259520 | bytes 10225664 | tf_op jit(solution)/shard_map/while/body/eval_jaxpr/hqsk,skd->qhd/dot_general | solution.py:79
  231.7 2.9 gather_fusion
  242.0 5.2 %fusion.41 = f32[128,4,128,1]{2,0,1,3:T(8,128)S(1)} fusion(f32[32,128,128,4]{2,1,3,0:T(8,128)} %copy-done, f32[4,128]{1,0:T(4,128)S(1)} %get-tuple-element.581, pred[128,32,128]{0,2,1:T(8,128)(4,1)S(1)} %or_and_fusion.2, bf16[32,128,128]{2,1,0:T(8,128)(2,1)S(1)} %gather_fusion.1), kind=kOutput, calls=%fused_computation.20.clone.1 | convolution fusion | flops 545259520 | bytes 10225664 | tf_op jit(solution)/shard_map/while/body/eval_jaxpr/hqsk,skd->qhd/dot_general | solution.py:79
  267.2 5.2 %fusion.41 = f32[128,4,128,1]{2,0,1,3:T(8,128)S(1)} fusion(f32[32,128,128,4]{2,1,3,0:T(8,128)} %copy-done, f32[4,128]{1,0:T(4,128)S(1)} %get-tuple-element.581, pred[128,32,128]{0,2,1:T(8,128)(4,1)S(1)} %or_and_fusion.2, bf16[32,128,128]{2,1,0:T(8,128)(2,1)S(1)} %gather_fusion.1), kind=kOutput, calls=%fused_computation.20.clone.1 | convolution fusion | flops 545259520 | bytes 10225664 | tf_op jit(solution)/shard_map/while/body/eval_jaxpr/hqsk,skd->qhd/dot_general | solution.py:79
  282.1 2.9 gather_fusion
  292.4 5.2 %fusion.41 = f32[128,4,128,1]{2,0,1,3:T(8,128)S(1)} fusion(f32[32,128,128,4]{2,1,3,0:T(8,128)} %copy-done, f32[4,128]{1,0:T(4,128)S(1)} %get-tuple-element.581, pred[128,32,128]{0,2,1:T(8,128)(4,1)S(1)} %or_and_fusion.2, bf16[32,128,128]{2,1,0:T(8,128)(2,1)S(1)} %gather_fusion.1), kind=kOutput, calls=%fused_computation.20.clone.1 | convolution fusion | flops 545259520 | bytes 10225664 | tf_op jit(solution)/shard_map/while/body/eval_jaxpr/hqsk,skd->qhd/dot_general | solution.py:79
  307.3 2.9 gather_fusion
  317.7 5.2 %fusion.41 = f32[128,4,128,1]{2,0,1,3:T(8,128)S(1)} fusion(f32[32,128,128,4]{2,1,3,0:T(8,128)} %copy-done, f32[4,128]{1,0:T(4,128)S(1)} %get-tuple-element.581, pred[128,32,128]{0,2,1:T(8,128)(4,1)S(1)} %or_and_fusion.2, bf16[32,128,128]{2,1,0:T(8,128)(2,1)S(1)} %gather_fusion.1), kind=kOutput, calls=%fused_computation.20.clone.1 | convolution fusion | flops 545259520 | bytes 10225664 | tf_op jit(solution)/shard_map/while/body/eval_jaxpr/hqsk,skd->qhd/dot_general | solution.py:79
  342.9 5.2 %fusion.41 = f32[128,4,128,1]{2,0,1,3:T(8,128)S(1)} fusion(f32[32,128,128,4]{2,1,3,0:T(8,128)} %copy-done, f32[4,128]{1,0:T(4,128)S(1)} %get-tuple-element.581, pred[128,32,128]{0,2,1:T(8,128)(4,1)S(1)} %or_and_fusion.2, bf16[32,128,128]{2,1,0:T(8,128)(2,1)S(1)} %gather_fusion.1), kind=kOutput, calls=%fused_computation.20.clone.1 | convolution fusion | flops 545259520 | bytes 10225664 | tf_op jit(solution)/shard_map/while/body/eval_jaxpr/hqsk,skd->qhd/dot_general | solution.py:79
  368.1 5.2 %fusion.41 = f32[128,4,128,1]{2,0,1,3:T(8,128)S(1)} fusion(f32[32,128,128,4]{2,1,3,0:T(8,128)} %copy-done, f32[4,128]{1,0:T(4,128)S(1)} %get-tuple-element.581, pred[128,32,128]{0,2,1:T(8,128)(4,1)S(1)} %or_and_fusion.2, bf16[32,128,128]{2,1,0:T(8,128)(2,1)S(1)} %gather_fusion.1), kind=kOutput, calls=%fused_computation.20.clone.1 | convolution fusion | flops 545259520 | bytes 10225664 | tf_op jit(solution)/shard_map/while/body/eval_jaxpr/hqsk,skd->qhd/dot_general | solution.py:79
  374.2 9.6 %all_gather.17 = f32[4,1024,4]{1,2,0:T(4,128)S(1)} all-gather(f32[1,1024,4]{1,2,0:T(4,128)S(1)} %bitcast.155), channel_id=1, replica_groups=mesh['pb'=64,'ka'=4] {'ka'}, dimensions={0}, use_global_device_ids=true | all-gather | bytes 81920 | tf_op jit(solution)/shard_map/all_gather | solution.py:15
  383.8 9.9 %all_gather.18 = f32[4,1024,4]{1,2,0:T(4,128)S(1)} all-gather(f32[1,1024,4]{1,2,0:T(4,128)S(1)} %bitcast.156), channel_id=1, replica_groups=mesh['pb'=64,'ka'=4] {'ka'}, dimensions={0}, use_global_device_ids=true | all-gather | bytes 81920 | tf_op jit(solution)/shard_map/all_gather | solution.py:15
  393.7 63.6 %all-gather.8.cloned.1.call-done = f32[4,1024,512]{2,1,0:T(8,128)} async-done(((f32[1,1024,512]{2,1,0:T(8,128)}), f32[4,1024,512]{2,1,0:T(8,128)}) %all-gather.8.cloned.1.call-update) | async-done | bytes 8388624 | tf_op jit(solution)/shard_map/all_gather | solution.py:15
  457.3 3.1 slice_bitcast_fusion
  460.5 22.8 %while.36 = (s32[]{:T(128)}, f32[1024,4]{0,1:T(4,128)S(1)}, f32[1024,4]{0,1:T(4,128)S(1)}, f32[1024,512]{1,0:T(8,128)}, f32[4,1024,4]{1,2,0:T(4,128)S(1)}, /*ind...) while((s32[]{:T(128)}, f32[1024,4]{0,1:T(4,128)S(1)}, ...), condition=%wide.region_5.6_spmd, body=%wide.region_4.5_spmd.sunk | while | flops 1597445 | bytes 14909591 | solution.py:21
  463.4 4.6 fusion.34
  471.0 4.6 fusion.34
  478.6 4.6 fusion.34
  (186 shorter events, 132.0 us)
Async XLA Ops:
  6.5 86.8 %all-gather.4.cloned.1.call-start = ((), (), s32[]{:S(2)}) async-start(), calls=%async_computation | async-start | bytes 4259840 | tf_op jit(solution)/shard_map/all_gather | solution.py:40
  7.3 165.1 %all-gather.6.cloned.1.call-start = ((), (), s32[]{:S(2)}) async-start(), calls=%async_computation.1 | async-start | bytes 4259840 | tf_op jit(solution)/shard_map/all_gather | solution.py:41
  8.0 449.3 %all-gather.8.cloned.1.call-start = ((), (), s32[]{:S(2)}) async-start(), calls=%async_computation.2 | async-start | bytes 10485760 | tf_op jit(solution)/shard_map/all_gather | solution.py:15
  185.4 3.2 copy-start
  210.6 3.2 copy-start
  235.8 3.2 copy-start
  261.1 3.2 copy-start
  286.3 3.2 copy-start
  311.5 3.2 copy-start
  336.7 3.2 copy-start
  361.9 3.2 copy-start
Sparse Core Ops, SparseCore 0:
  10.1 83.1 all-gather.3
  96.1 76.2 all-gather.5
  374.3 82.9 all-gather.7
where the time goes:
time: 494 us; the launch traced here: 492 us
  waiting for transfers between devices  229 us (46%)
  local copies, waits for them, and re-layouts  101 us (20%)
  other arithmetic  51.8 us (10%)
  matrix products  51.4 us (10%)
  loops' own time  26.3 us (5%)
  blocking collectives  19.5 us (4%)
  between operations  13.1 us (3%)
    all_gather x1, waiting for transfers between devices, shards(): lax.all_gather(key_cache, 'pb', axis=0, tiled=True)  85.3 us
    all_gather x1, waiting for transfers between devices, shards(): lax.all_gather(value_cache, 'pb', axis=0, tiled=True)  79.1 us
    all_gather x1, waiting for transfers between devices, merged(): everything = jax.tree.map(lambda part: lax.all_gather(part, axis), shard)  63.6 us
    dot_general x8, matrix products, one_block(): jnp.einsum('hqsk,skd->qhd', weights.astype(jnp.bfloat16), value_tiles, pr...  41.5 us
    another operation x1, loops' own time, shards(): lax.map(one_block, jnp.arange(local_blocks, dtype=jnp.int32))  26.2 us
    gather x8, local copies, waits for them, and re-layouts, one_block(): key_tiles = all_key_tiles[picked]  23.5 us
    gather x8, local copies, waits for them, and re-layouts, one_block(): value_tiles = all_value_tiles[picked]  23.5 us
    all_gather x2, blocking collectives, merged(): everything = jax.tree.map(lambda part: lax.all_gather(part, axis), shard)  19.5 us
  transfers between devices with their start and end apart: 3, of which 3 were waited for; matrix products, arithmetic and copies ran while one was open for 0% of the time, Pallas kernels for 0%

commit v1 on v0

--- a/solution.py
+++ b/solution.py
@@ -38,7 +38,15 @@
 def shards(queries, key_cache, value_cache, block_list, block_count):
     shard_keys, shard_values = (
         lax.all_gather(key_cache, "pb", axis=0, tiled=True),
-        lax.all_gather(value_cache, "pb", axis=0, tiled=True),
+        jnp.concatenate(
+            jax.lax.all_to_all(
+                jnp.stack([value_cache for _ in range(jax.lax.axis_size("pb"))]),
+                axis_name="pb",
+                split_axis=0,
+                concat_axis=0,
+            ),
+            axis=0,
+        ),
     )
     group_index = lax.axis_index("pb")
     shard_index = lax.axis_index("ka")

time: 494 us -> 449 us (0.909)
  waiting for transfers between devices: 229 us -> 173 us
  starting transfers between devices: 0.08 us -> 13.4 us
    all_gather x1 -> x0, waiting for transfers between devices: 79.1 us -> none  [shards(): lax.all_gather(value_cache, 'pb', axis=0, tiled=True)]
    all_to_all x0 -> x1, waiting for transfers between devices: none -> 16.6 us  [shards(): jax.lax.all_to_all(jnp.stack([value_cache for _ in range(jax.lax.axis_siz...]
    all_to_all x0 -> x1, starting transfers between devices: none -> 13.3 us  [shards(): jax.lax.all_to_all(jnp.stack([value_cache for _ in range(jax.lax.axis_siz...]
    dynamic_slice x8, local copies, waits for them, and re-layouts: 10.5 us -> 5.22 us  [one_block(): lax.dynamic_index_in_dim(block_count, block_pos, 0, keepdims=False)]
  transfers between devices with their start and end apart: 3 -> 3, of which waited for: 3 -> 3; matrix products, arithmetic and copies ran while one was open for 0% -> 1% of each run, Pallas kernels for 0% -> 0%
where the time goes in v1:
time: 449 us; the launch traced here: 447 us
  waiting for transfers between devices  173 us (39%)
  local copies, waits for them, and re-layouts  99.1 us (22%)
  other arithmetic  51.8 us (12%)
  matrix products  51.4 us (11%)
  loops' own time  26.3 us (6%)
  blocking collectives  19 us (4%)
  between operations  13.5 us (3%)
  starting transfers between devices  13.4 us (3%)
    all_gather x1, waiting for transfers between devices, shards(): lax.all_gather(key_cache, 'pb', axis=0, tiled=True)  90.1 us
    all_gather x1, waiting for transfers between devices, merged(): everything = jax.tree.map(lambda part: lax.all_gather(part, axis), shard)  65.2 us
    dot_general x8, matrix products, one_block(): jnp.einsum('hqsk,skd->qhd', weights.astype(jnp.bfloat16), value_tiles, pr...  41.5 us
    another operation x1, loops' own time, shards(): lax.map(one_block, jnp.arange(local_blocks, dtype=jnp.int32))  26.2 us
    gather x8, local copies, waits for them, and re-layouts, one_block(): key_tiles = all_key_tiles[picked]  23.5 us
    gather x8, local copies, waits for them, and re-layouts, one_block(): value_tiles = all_value_tiles[picked]  23.5 us
    all_gather x2, blocking collectives, merged(): everything = jax.tree.map(lambda part: lax.all_gather(part, axis), shard)  19 us
    all_to_all x1, waiting for transfers between devices, shards(): jax.lax.all_to_all(jnp.stack([value_cache for _ in range(jax.lax.axis_siz...  16.6 us
  transfers between devices with their start and end apart: 3, of which 3 were waited for; matrix products, arithmetic and copies ran while one was open for 1% of the time, Pallas kernels for 0%

profile of v1, /device:TPU:1, one launch (start us, length us, event | category | flops | bytes accessed | tf_op | source)
XLA Modules:
  0.0 446.9 jit_solution(2412707682118810137)
XLA Ops:
  7.3 3.8 stack.2
  11.1 13.3 %all-to-all-start = ((bf16[64,256,128]{2,1,0:T(8,128)(2,1)}), bf16[64,256,128]{2,1,0:T(8,128)(2,1)}, u32[]{:S(2)}, u32[]{:S(2)}) async-start(bf16[64,256,128]{2,1,0:T(8,128)(2,1)} %stack.2), calls=%async_computation | async-start | bytes 8388608 | tf_op jit(solution)/shard_map/all_to_all | solution.py:42
  24.5 90.1 %all-gather.3.cloned.1.call-done = bf16[16384,128]{1,0:T(8,128)(2,1)} async-done(((bf16[256,128]{1,0:T(8,128)(2,1)}), bf16[16384,128]{1,0:T(8,128)(2,1)}) %all-gather.3.cloned.1.call-update) | async-done | bytes 4194320 | tf_op jit(solution)/shard_map/all_gather | solution.py:40
  114.5 16.6 %all-to-all-done = bf16[64,256,128]{2,1,0:T(8,128)(2,1)} async-done(((bf16[64,256,128]{2,1,0:T(8,128)(2,1)}), bf16[64,256,128]{2,1,0:T(8,128)(2,1)}, u32[]{:S(2)}, u32[]{:S(2)}) %all-to-all-start) | async-done | bytes 4194336 | tf_op jit(solution)/shard_map/all_to_all | solution.py:42
  131.1 196.5 %while.37 = (s32[]{:T(128)}, f32[8,128,4]{1,2,0:T(4,128)S(1)}, f32[8,128,4]{1,2,0:T(4,128)S(1)}, f32[8,128,512]{2,1,0:T(8,128)}, s32[8]{0:T(128)S(1)}, /*index=5...) while((s32[]{:T(128)}, f32[8,128,4]{1,2,0:T(4,128)S(1)}, ...), condition=%wide.region_3.4_spmd.clone, body=%wide.region_0.3_spmd.clone.sunk | while | flops 1098400256 | bytes 69129872 | solution.py:95
  139.2 2.9 gather_fusion
  149.6 5.2 %fusion.41 = f32[128,4,128,1]{2,0,1,3:T(8,128)S(1)} fusion(f32[32,128,128,4]{2,1,3,0:T(8,128)} %copy-done, f32[4,128]{1,0:T(4,128)S(1)} %get-tuple-element.581, pred[128,32,128]{0,2,1:T(8,128)(4,1)S(1)} %or_and_fusion.2, bf16[32,128,128]{2,1,0:T(8,128)(2,1)S(1)} %gather_fusion.1), kind=kOutput, calls=%fused_computation.20.clone.1 | convolution fusion | flops 545259520 | bytes 10225664 | tf_op jit(solution)/shard_map/while/body/eval_jaxpr/hqsk,skd->qhd/dot_general | solution.py:87
  174.2 5.2 %fusion.41 = f32[128,4,128,1]{2,0,1,3:T(8,128)S(1)} fusion(f32[32,128,128,4]{2,1,3,0:T(8,128)} %copy-done, f32[4,128]{1,0:T(4,128)S(1)} %get-tuple-element.581, pred[128,32,128]{0,2,1:T(8,128)(4,1)S(1)} %or_and_fusion.2, bf16[32,128,128]{2,1,0:T(8,128)(2,1)S(1)} %gather_fusion.1), kind=kOutput, calls=%fused_computation.20.clone.1 | convolution fusion | flops 545259520 | bytes 10225664 | tf_op jit(solution)/shard_map/while/body/eval_jaxpr/hqsk,skd->qhd/dot_general | solution.py:87
  188.4 2.9 gather_fusion
  198.7 5.2 %fusion.41 = f32[128,4,128,1]{2,0,1,3:T(8,128)S(1)} fusion(f32[32,128,128,4]{2,1,3,0:T(8,128)} %copy-done, f32[4,128]{1,0:T(4,128)S(1)} %get-tuple-element.581, pred[128,32,128]{0,2,1:T(8,128)(4,1)S(1)} %or_and_fusion.2, bf16[32,128,128]{2,1,0:T(8,128)(2,1)S(1)} %gather_fusion.1), kind=kOutput, calls=%fused_computation.20.clone.1 | convolution fusion | flops 545259520 | bytes 10225664 | tf_op jit(solution)/shard_map/while/body/eval_jaxpr/hqsk,skd->qhd/dot_general | solution.py:87
  223.3 5.2 %fusion.41 = f32[128,4,128,1]{2,0,1,3:T(8,128)S(1)} fusion(f32[32,128,128,4]{2,1,3,0:T(8,128)} %copy-done, f32[4,128]{1,0:T(4,128)S(1)} %get-tuple-element.581, pred[128,32,128]{0,2,1:T(8,128)(4,1)S(1)} %or_and_fusion.2, bf16[32,128,128]{2,1,0:T(8,128)(2,1)S(1)} %gather_fusion.1), kind=kOutput, calls=%fused_computation.20.clone.1 | convolution fusion | flops 545259520 | bytes 10225664 | tf_op jit(solution)/shard_map/while/body/eval_jaxpr/hqsk,skd->qhd/dot_general | solution.py:87
  237.5 2.9 gather_fusion
  247.8 5.2 %fusion.41 = f32[128,4,128,1]{2,0,1,3:T(8,128)S(1)} fusion(f32[32,128,128,4]{2,1,3,0:T(8,128)} %copy-done, f32[4,128]{1,0:T(4,128)S(1)} %get-tuple-element.581, pred[128,32,128]{0,2,1:T(8,128)(4,1)S(1)} %or_and_fusion.2, bf16[32,128,128]{2,1,0:T(8,128)(2,1)S(1)} %gather_fusion.1), kind=kOutput, calls=%fused_computation.20.clone.1 | convolution fusion | flops 545259520 | bytes 10225664 | tf_op jit(solution)/shard_map/while/body/eval_jaxpr/hqsk,skd->qhd/dot_general | solution.py:87
  272.4 5.2 %fusion.41 = f32[128,4,128,1]{2,0,1,3:T(8,128)S(1)} fusion(f32[32,128,128,4]{2,1,3,0:T(8,128)} %copy-done, f32[4,128]{1,0:T(4,128)S(1)} %get-tuple-element.581, pred[128,32,128]{0,2,1:T(8,128)(4,1)S(1)} %or_and_fusion.2, bf16[32,128,128]{2,1,0:T(8,128)(2,1)S(1)} %gather_fusion.1), kind=kOutput, calls=%fused_computation.20.clone.1 | convolution fusion | flops 545259520 | bytes 10225664 | tf_op jit(solution)/shard_map/while/body/eval_jaxpr/hqsk,skd->qhd/dot_general | solution.py:87
  297.0 5.2 %fusion.41 = f32[128,4,128,1]{2,0,1,3:T(8,128)S(1)} fusion(f32[32,128,128,4]{2,1,3,0:T(8,128)} %copy-done, f32[4,128]{1,0:T(4,128)S(1)} %get-tuple-element.581, pred[128,32,128]{0,2,1:T(8,128)(4,1)S(1)} %or_and_fusion.2, bf16[32,128,128]{2,1,0:T(8,128)(2,1)S(1)} %gather_fusion.1), kind=kOutput, calls=%fused_computation.20.clone.1 | convolution fusion | flops 545259520 | bytes 10225664 | tf_op jit(solution)/shard_map/while/body/eval_jaxpr/hqsk,skd->qhd/dot_general | solution.py:87
  321.6 5.2 %fusion.41 = f32[128,4,128,1]{2,0,1,3:T(8,128)S(1)} fusion(f32[32,128,128,4]{2,1,3,0:T(8,128)} %copy-done, f32[4,128]{1,0:T(4,128)S(1)} %get-tuple-element.581, pred[128,32,128]{0,2,1:T(8,128)(4,1)S(1)} %or_and_fusion.2, bf16[32,128,128]{2,1,0:T(8,128)(2,1)S(1)} %gather_fusion.1), kind=kOutput, calls=%fused_computation.20.clone.1 | convolution fusion | flops 545259520 | bytes 10225664 | tf_op jit(solution)/shard_map/while/body/eval_jaxpr/hqsk,skd->qhd/dot_general | solution.py:87
  327.6 9.5 %all_gather.13 = f32[4,1024,4]{1,2,0:T(4,128)S(1)} all-gather(f32[1,1024,4]{1,2,0:T(4,128)S(1)} %bitcast.154), channel_id=1, replica_groups=mesh['pb'=64,'ka'=4] {'ka'}, dimensions={0}, use_global_device_ids=true | all-gather | bytes 81920 | tf_op jit(solution)/shard_map/all_gather | solution.py:15
  337.1 9.5 %all_gather.14 = f32[4,1024,4]{1,2,0:T(4,128)S(1)} all-gather(f32[1,1024,4]{1,2,0:T(4,128)S(1)} %bitcast.155), channel_id=1, replica_groups=mesh['pb'=64,'ka'=4] {'ka'}, dimensions={0}, use_global_device_ids=true | all-gather | bytes 81920 | tf_op jit(solution)/shard_map/all_gather | solution.py:15
  346.7 65.2 %all-gather.5.cloned.1.call-done = f32[4,1024,512]{2,1,0:T(8,128)} async-done(((f32[1,1024,512]{2,1,0:T(8,128)}), f32[4,1024,512]{2,1,0:T(8,128)}) %all-gather.5.cloned.1.call-update) | async-done | bytes 8388624 | tf_op jit(solution)/shard_map/all_gather | solution.py:15
  411.9 3.1 slice_bitcast_fusion
  415.0 22.8 %while.36 = (s32[]{:T(128)}, f32[1024,4]{0,1:T(4,128)S(1)}, f32[1024,4]{0,1:T(4,128)S(1)}, f32[1024,512]{1,0:T(8,128)}, f32[4,1024,4]{1,2,0:T(4,128)S(1)}, /*ind...) while((s32[]{:T(128)}, f32[1024,4]{0,1:T(4,128)S(1)}, ...), condition=%wide.region_5.6_spmd, body=%wide.region_4.5_spmd.sunk | while | flops 1597445 | bytes 14909591 | solution.py:21
  418.0 4.6 %fusion.34 = f32[1024,512]{1,0:T(8,128)} fusion(f32[128,8,4,128]{3,2,1,0:T(4,128)S(1)} %bitcast.147, f32[1024,512]{1,0:T(8,128)} %get-tuple-element.648, f32[128,8,4,128]{3,2,1,0:T(4,128)S(1)} %bitcast.148, f32[4,1024,512]{2,1,0:T(8,128)} %get-tuple-element.661, s32[]{:T(128)S(6)} %select_n.78), kind=kLoop, calls=%fused_computation.5.clone.1 | loop fusion | flops 1572864 | bytes 10485764 | tf_op jit(solution)/shard_map/while/body/eval_jaxpr/add | solution.py:32
  425.5 4.6 %fusion.34 = f32[1024,512]{1,0:T(8,128)} fusion(f32[128,8,4,128]{3,2,1,0:T(4,128)S(1)} %bitcast.147, f32[1024,512]{1,0:T(8,128)} %get-tuple-element.648, f32[128,8,4,128]{3,2,1,0:T(4,128)S(1)} %bitcast.148, f32[4,1024,512]{2,1,0:T(8,128)} %get-tuple-element.661, s32[]{:T(128)S(6)} %select_n.78), kind=kLoop, calls=%fused_computation.5.clone.1 | loop fusion | flops 1572864 | bytes 10485764 | tf_op jit(solution)/shard_map/while/body/eval_jaxpr/add | solution.py:32
  433.1 4.6 %fusion.34 = f32[1024,512]{1,0:T(8,128)} fusion(f32[128,8,4,128]{3,2,1,0:T(4,128)S(1)} %bitcast.147, f32[1024,512]{1,0:T(8,128)} %get-tuple-element.648, f32[128,8,4,128]{3,2,1,0:T(4,128)S(1)} %bitcast.148, f32[4,1024,512]{2,1,0:T(8,128)} %get-tuple-element.661, s32[]{:T(128)S(6)} %select_n.78), kind=kLoop, calls=%fused_computation.5.clone.1 | loop fusion | flops 1572864 | bytes 10485764 | tf_op jit(solution)/shard_map/while/body/eval_jaxpr/add | solution.py:32
  (188 shorter events, 132.0 us)
Async XLA Ops:
  6.5 108.0 %all-gather.3.cloned.1.call-start = ((), (), s32[]{:S(2)}) async-start(), calls=%async_computation.1 | async-start | bytes 4259840 | tf_op jit(solution)/shard_map/all_gather | solution.py:40
  11.1 120.0 %copy-start.1 = (s32[8]{0:T(128)S(1)}, s32[8]{0:T(128)}, u32[]{:S(2)}) copy-start(s32[8]{0:T(128)} %param.13) | copy-start | bytes 100
  11.1 120.0 %all-to-all-start = ((bf16[64,256,128]{2,1,0:T(8,128)(2,1)}), bf16[64,256,128]{2,1,0:T(8,128)(2,1)}, u32[]{:S(2)}, u32[]{:S(2)}) async-start(bf16[64,256,128]{2,1,0:T(8,128)(2,1)} %stack.2), calls=%async_computation | async-start | bytes 8388608 | tf_op jit(solution)/shard_map/all_to_all | solution.py:42
  24.4 387.5 %all-gather.5.cloned.1.call-start = ((), (), s32[]{:S(2)}) async-start(), calls=%async_computation.2 | async-start | bytes 10485760 | tf_op jit(solution)/shard_map/all_gather | solution.py:15
  143.4 3.2 copy-start
  168.0 3.2 copy-start
  192.6 3.2 copy-start
  217.1 3.2 copy-start
  241.7 3.2 copy-start
  266.2 3.2 copy-start
  290.8 3.2 copy-start
  315.4 3.2 copy-start
Sparse Core Ops, SparseCore 0:
  10.1 104.3 all-gather.2
  327.8 84.0 all-gather.4
